TPU v7x, 512 devices: a whole 4x4x16 slice. The times are simulated.
512 devices in a mesh: ka: 8 (over x, core), dev: 64 (over z, y).
Axes of the slice: x: 4, y: 4, z: 16, core: 2. Of those that a mesh axis runs over, the one named last changes fastest.
Arguments:
- density: float32 [4096, 2048], P('dev'), may hold values from 0 to 1
- fields_fwd: bfloat16 [8, 6, 4096, 2048], P('ka', None, 'dev'), may hold values from -0.796875 to 0.796875
- fields_adj: bfloat16 [8, 6, 4096, 2048], P('ka', None, 'dev'), may hold values from -0.796875 to 0.796875
- filter_band: float32 [4096, 17], replicated, may hold values from 0.2 to 1
- k_weights: float32 [8], replicated, may hold values from 0.3 to 3
- kpoint_ids: int32 [8], replicated, may hold values from 0 to 7, each once
Outputs:
- projected: float32 [4096, 2048], P('dev')
- design_grad: float32 [4096, 2048], P('dev')
All inputs are finite; a program needn't handle non-finite values.
Results may differ from a plain program's by a relative error of at most 0.0003.
Values sent between devices are 32-bit elements; how exact they have to be, the bound alone decides.
A program may use at most 64 MiB of HBM per device.

v0:
```python
import jax
import jax.numpy as jnp
from jax import lax
from jax.sharding import PartitionSpec as P


def padded(block, sides, width):
    for axis, dim in sides:
        count = lax.axis_size(axis)
        forward = [(i, i + 1) for i in range(count - 1)]
        backward = [(target, source) for source, target in forward]
        low = lax.ppermute(
            lax.slice_in_dim(block, block.shape[dim] - width, None, axis=dim), axis, forward
        )
        high = lax.ppermute(lax.slice_in_dim(block, 0, width, axis=dim), axis, backward)
        block = jnp.concatenate([low, block, high], axis=dim)
    return block


def project(filtered):
    beta = 8.0
    eta = 0.5
    quot = jnp.tanh(beta * eta) + jnp.tanh(beta * (1.0 - eta))
    inner = jnp.tanh(beta * (filtered - eta))
    return ((jnp.tanh(beta * eta) + inner) / quot, beta * (1.0 - inner * inner) / quot)


def transpose_filter(extended, band_local, rows, radius):
    taps = band_local.shape[1]
    total = jnp.zeros((rows, extended.shape[1]), jnp.float32)
    for j in range(taps):
        lower = 2 * radius - j
        total = (
            total + band_local[lower : lower + rows, j][:, None] * extended[lower : lower + rows]
        )
    return total


def shards(density, fields_fwd, fields_adj, filter_band, k_weights, kpoint_ids):
    rows, cols = density.shape
    taps = filter_band.shape[1]
    radius = (taps - 1) // 2
    band = filter_band / jnp.sum(filter_band, axis=1, keepdims=True)
    row_start = lax.axis_index("dev") * rows
    band_padded = jnp.pad(band, ((radius, radius), (0, 0)))
    band_local = lax.dynamic_slice_in_dim(band_padded, row_start, rows + 2 * radius, 0)
    extended = padded(density, (("dev", 0),), radius)
    filtered = jnp.zeros_like(density)
    for j in range(taps):
        filtered = (
            filtered + band_local[radius : radius + rows, j][:, None] * extended[j : j + rows]
        )
    projected, slope = project(filtered)
    kloc = fields_fwd.shape[0]
    kcount = k_weights.shape[0]
    slots = jnp.arange(kcount, dtype=jnp.int32)
    global_k = lax.axis_index("ka") * kloc + jnp.arange(kloc, dtype=jnp.int32)
    chosen = jnp.sum(
        (global_k[:, None] == slots[None, :]).astype(jnp.int32) * kpoint_ids[None, :], axis=1
    )
    weight = jnp.sum(
        (chosen[:, None] == slots[None, :]).astype(jnp.float32) * k_weights[None, :], axis=1
    )
    prod = fields_fwd[0].astype(jnp.float32) * fields_adj[0].astype(jnp.float32)
    term = jnp.sum(prod[0:3], axis=0) - jnp.sum(prod[3:6], axis=0)
    sens_local = weight[0] * term
    sens = lax.psum(sens_local, "ka")
    grad_filtered = 11.1 * slope * sens
    grad_ext = padded(grad_filtered, (("dev", 0),), radius)
    design_grad = transpose_filter(grad_ext, band_local, rows, radius)
    return (projected, design_grad)


def solution(mesh):
    return jax.shard_map(
        shards,
        mesh=mesh,
        in_specs=(
            P("dev", None),
            P("ka", None, "dev", None),
            P("ka", None, "dev", None),
            P(),
            P(),
            P(),
        ),
        out_specs=(P("dev", None), P("dev", None)),
        check_vma=False,
    )
```

profile of v0, /device:TPU:120, one launch (start us, length us, event | category | flops | bytes accessed | tf_op | source)
XLA Modules:
  0.0 119.0 jit_solution(11204316366250120609)
XLA Ops:
  7.2 0.0 all-reduce.3.cloned.1.call-start
  7.2 2.5 %convert_multiply_fusion = f32[1,6,64,2048]{3,2,1,0:T(8,128)S(1)} fusion(bf16[1,6,64,2048]{3,2,1,0:T(8,128)(2,1)} %param.8, bf16[1,6,64,2048]{3,2,1,0:T(8,128)(2,1)} %param.7), kind=kLoop, calls=%fused_computation | loop fusion | flops 2359296 | bytes 6291456 | tf_op jit(solution)/shard_map/mul | solution.py:64
  9.7 0.0 copy-start.2
  9.7 0.0 copy-start.3
  9.7 0.2 slice_reduce_fusion
  10.0 0.0 copy-start
  10.0 0.0 copy-start.1
  10.0 0.4 copy-done.2
  10.4 0.6 fusion.65
  11.0 0.0 copy-done.3
  11.0 1.2 %fusion.66 = f32[]{:T(128)} fusion(f32[8]{0:T(128)S(1)} %copy-done.3, s32[]{:T(128)} %fusion.65), kind=kLoop, calls=%fused_computation.125 | loop fusion | flops 23 | bytes 40 | tf_op jit(solution)/shard_map/reduce_sum | solution.py:61
  12.2 1.5 %subtract_multiply_fusion = f32[64,2048]{1,0:T(8,128)} fusion(f32[64,2048]{1,0:T(8,128)S(1)} %get-tuple-element.3, f32[64,2048]{1,0:T(8,128)S(1)} %get-tuple-element.2, f32[]{:T(128)} %fusion.66), kind=kLoop, calls=%fused_computation.114 | loop fusion | flops 262144 | bytes 1572868 | tf_op jit(solution)/shard_map/mul | solution.py:66
  13.7 0.0 all-reduce.3.cloned.1.call-update
  13.8 0.0 copy-done
  13.8 4.7 %collective-permute-start = (f32[8,2048]{1,0:T(8,128)S(1)}, f32[8,2048]{1,0:T(8,128)S(1)}, u32[]{:S(2)}, u32[]{:S(2)}) collective-permute-start(f32[8,2048]{1,0:T(8,128)S(1)} %get-tuple-element.10), channel_id=1, source_target_pairs={{0,1},{1,2},{2,3},{3,4},{4,5},{5,6},{6,7},{7,8},{8,9},{9,10},{10,1... | collective-permute-start | bytes 196616 | tf_op jit(solution)/shard_map/ppermute | solution.py:12
  18.5 1.9 %collective-permute-start.1 = (f32[8,2048]{1,0:T(8,128)S(1)}, f32[8,2048]{1,0:T(8,128)S(1)}, u32[]{:S(2)}, u32[]{:S(2)}) collective-permute-start(f32[8,2048]{1,0:T(8,128)S(1)} %get-tuple-element.11), channel_id=1, source_target_pairs={{1,0},{2,1},{3,2},{4,3},{5,4},{6,5},{7,6},{8,7},{9,8},{10,9},{11,1... | collective-permute-start | bytes 196616 | tf_op jit(solution)/shard_map/ppermute | solution.py:15
  20.4 0.0 copy-done.1
  20.4 0.1 reduce_sum.45
  20.5 0.2 dynamic-slice_bitcast_fusion.15
  20.7 0.2 dynamic-slice_bitcast_fusion.14
  20.9 0.0 collective-permute-done
  20.9 0.1 constant_dynamic-update-slice_fusion
  21.0 6.9 %collective-permute-done.1 = f32[8,2048]{1,0:T(8,128)S(1)} collective-permute-done((f32[8,2048]{1,0:T(8,128)S(1)}, f32[8,2048]{1,0:T(8,128)S(1)}, u32[]{:S(2)}, u32[]{:S(2)}) %collective-permute-start.1) | collective-permute-done | bytes 65568 | tf_op jit(solution)/shard_map/ppermute | solution.py:15
  28.0 65.1 %all-reduce.3.cloned.1.call-done = f32[64,2048]{1,0:T(8,128)} async-done(((f32[64,2048]{1,0:T(8,128)}), f32[64,2048]{1,0:T(8,128)}) %all-reduce.3.cloned.1.call-update) | async-done | bytes 524304 | tf_op jit(solution)/shard_map/psum | solution.py:67
  93.0 2.3 %multiply_multiply_fusion = (f32[64,2048]{1,0:T(8,128)S(1)}, f32[64,2048]{1,0:T(8,128)S(1)}) fusion(f32[64,2048]{1,0:T(8,128)} %all-reduce.3.cloned.1.call-done, f32[72,2048]{1,0:T(8,128)S(1)} %constant_dynamic-update-slice_fusion.2, f32[64]{0:T(128)S(1)} %get-tuple-element.36, f32[64]{0:T(128)S(1)} %get-tuple-element.21, f32[64]{0:T(128)S(1)} %get-tuple-element.22, ...), kind=kLoop, calls=%fused_computation.115 | loop fusion | flops 5111808 | bytes 10490112 | tf_op jit(solution)/shard_map/mul | solution.py:68
  95.4 4.6 %collective-permute-start.3 = (f32[8,2048]{1,0:T(8,128)S(1)}, f32[8,2048]{1,0:T(8,128)S(1)}, u32[]{:S(2)}, u32[]{:S(2)}) collective-permute-start(f32[8,2048]{1,0:T(8,128)S(1)} %get-tuple-element.7), channel_id=1, source_target_pairs={{0,1},{1,2},{2,3},{3,4},{4,5},{5,6},{6,7},{7,8},{8,9},{9,10},{10,1... | collective-permute-start | bytes 196616 | tf_op jit(solution)/shard_map/ppermute | solution.py:12
  100.0 1.9 %collective-permute-start.2 = (f32[8,2048]{1,0:T(8,128)S(1)}, f32[8,2048]{1,0:T(8,128)S(1)}, u32[]{:S(2)}, u32[]{:S(2)}) collective-permute-start(f32[8,2048]{1,0:T(8,128)S(1)} %get-tuple-element.6), channel_id=1, source_target_pairs={{1,0},{2,1},{3,2},{4,3},{5,4},{6,5},{7,6},{8,7},{9,8},{10,9},{11,1... | collective-permute-start | bytes 196616 | tf_op jit(solution)/shard_map/ppermute | solution.py:15
  101.9 0.9 add_multiply_fusion
  102.8 0.0 collective-permute-done.3
  102.8 6.7 %collective-permute-done.2 = f32[8,2048]{1,0:T(8,128)S(1)} collective-permute-done((f32[8,2048]{1,0:T(8,128)S(1)}, f32[8,2048]{1,0:T(8,128)S(1)}, u32[]{:S(2)}, u32[]{:S(2)}) %collective-permute-start.2) | collective-permute-done | bytes 65568 | tf_op jit(solution)/shard_map/ppermute | solution.py:15
  109.4 2.7 %fusion.3 = f32[64,2048]{1,0:T(8,128)} fusion(f32[64,2048]{1,0:T(8,128)S(1)} %get-tuple-element.4, f32[8,2048]{1,0:T(8,128)S(1)} %collective-permute-done.3, f32[8,2048]{1,0:T(8,128)S(1)} %collective-permute-done.2, f32[64]{0:T(128)S(1)} %get-tuple-element.44, f32[64]{0:T(128)S(1)} %get-tuple-element.13, f32[64]{0:T(128)S(1)} %get-tuple-element.14, ...), kind=kLoop, calls=%fused_computation.34 | loop fusion | flops 6422528 | bytes 1184000 | tf_op jit(solution)/shard_map/add | solution.py:34
  (5 shorter events, 0.1 us)
Async XLA Ops:
  7.2 85.9 %all-reduce.3.cloned.1.call-start = ((), (), s32[]{:S(2)}) async-start(), calls=%async_computation | async-start | bytes 1048576 | tf_op jit(solution)/shard_map/psum | solution.py:67
  9.7 0.7 copy-start.2
  9.7 1.3 %copy-start.3 = (f32[8]{0:T(128)S(1)}, f32[8]{0:T(128)}, u32[]{:S(2)}) copy-start(f32[8]{0:T(128)} %param.10) | copy-start | bytes 100
  10.0 3.8 %copy-start = (f32[64,2048]{1,0:T(8,128)S(1)}, f32[64,2048]{1,0:T(8,128)}, u32[]{:S(2)}) copy-start(f32[64,2048]{1,0:T(8,128)} %param.6) | copy-start | bytes 1572868
  10.0 10.5 %copy-start.1 = (f32[4096,17]{0,1:T(8,128)S(1)}, f32[4096,17]{0,1:T(8,128)}, u32[]{:S(2)}) copy-start(f32[4096,17]{0,1:T(8,128)} %param.9) | copy-start | bytes 835588
  13.8 7.1 %collective-permute-start = (f32[8,2048]{1,0:T(8,128)S(1)}, f32[8,2048]{1,0:T(8,128)S(1)}, u32[]{:S(2)}, u32[]{:S(2)}) collective-permute-start(f32[8,2048]{1,0:T(8,128)S(1)} %get-tuple-element.10), channel_id=1, source_target_pairs={{0,1},{1,2},{2,3},{3,4},{4,5},{5,6},{6,7},{7,8},{8,9},{9,10},{10,1... | collective-permute-start | bytes 196616 | tf_op jit(solution)/shard_map/ppermute | solution.py:12
  18.5 9.5 %collective-permute-start.1 = (f32[8,2048]{1,0:T(8,128)S(1)}, f32[8,2048]{1,0:T(8,128)S(1)}, u32[]{:S(2)}, u32[]{:S(2)}) collective-permute-start(f32[8,2048]{1,0:T(8,128)S(1)} %get-tuple-element.11), channel_id=1, source_target_pairs={{1,0},{2,1},{3,2},{4,3},{5,4},{6,5},{7,6},{8,7},{9,8},{10,9},{11,1... | collective-permute-start | bytes 196616 | tf_op jit(solution)/shard_map/ppermute | solution.py:15
  95.4 7.4 %collective-permute-start.3 = (f32[8,2048]{1,0:T(8,128)S(1)}, f32[8,2048]{1,0:T(8,128)S(1)}, u32[]{:S(2)}, u32[]{:S(2)}) collective-permute-start(f32[8,2048]{1,0:T(8,128)S(1)} %get-tuple-element.7), channel_id=1, source_target_pairs={{0,1},{1,2},{2,3},{3,4},{4,5},{5,6},{6,7},{7,8},{8,9},{9,10},{10,1... | collective-permute-start | bytes 196616 | tf_op jit(solution)/shard_map/ppermute | solution.py:12
  100.0 9.5 %collective-permute-start.2 = (f32[8,2048]{1,0:T(8,128)S(1)}, f32[8,2048]{1,0:T(8,128)S(1)}, u32[]{:S(2)}, u32[]{:S(2)}) collective-permute-start(f32[8,2048]{1,0:T(8,128)S(1)} %get-tuple-element.6), channel_id=1, source_target_pairs={{1,0},{2,1},{3,2},{4,3},{5,4},{6,5},{7,6},{8,7},{9,8},{10,9},{11,1... | collective-permute-start | bytes 196616 | tf_op jit(solution)/shard_map/ppermute | solution.py:15
Sparse Core Ops, SparseCore 0:
  13.9 79.1 all-reduce.2
where the time goes:
time: 119 us
  waiting for transfers between devices  78.7 us (66%)
  between operations  14.2 us (12%)
  starting transfers between devices  13.2 us (11%)
  other arithmetic  12 us (10%)
    psum x1, waiting for transfers between devices, shards(): sens = lax.psum(sens_local, 'ka')  65.1 us
    ppermute x2, waiting for transfers between devices, padded(): lax.ppermute(lax.slice_in_dim(block, 0, width, axis=dim), axis, backward)  13.6 us
    ppermute x2, starting transfers between devices, padded(): lax.ppermute(lax.slice_in_dim(block, block.shape[dim] - width, None, axis...  9.3 us
    ppermute x2, starting transfers between devices, padded(): lax.ppermute(lax.slice_in_dim(block, 0, width, axis=dim), axis, backward)  3.84 us
    add x1, other arithmetic, transpose_filter(): total + band_local[lower:lower + rows, j][:, None] * extended[lower:lower...  2.68 us
    mul x1, other arithmetic, shards(): prod = fields_fwd[0].astype(jnp.float32) * fields_adj[0].astype(jnp.float32)  2.47 us
  transfers between devices with their start and end apart: 5, of which 3 were waited for; matrix products, arithmetic and copies ran while one was open for 1% of the time, Pallas kernels for 0%

commit v1 on v0

v1 whole, which is shorter than its diff:
```python
import functools

import jax
import jax.numpy as jnp
from jax import lax
from jax.experimental import pallas as pl
from jax.experimental.pallas import tpu as pltpu
from jax.sharding import PartitionSpec as P

MESH = pl.DeviceIdType.MESH
BETA, ETA = 8.0, 0.5


def split(value):
    high = value.astype(jnp.bfloat16)
    low = (value - high.astype(jnp.float32)).astype(jnp.bfloat16)
    return high, low


def kernel(
    sizes,
    density, fwd, adj, band_t, weights, ids,
    projected, design,
    fwd_buf, adj_buf, ext, band_buf, band_rows, mat, mat_t, inner_buf, weight_buf, id_buf,
    mine, pair_in, part, relay_in, direct_in, halo_out, halo_in, gather,
    field_sem, small_sem, barrier_send, barrier_recv,
    pair_send, pair_recv, ring_send, ring_recv, edge_send, edge_recv, out_send, out_recv,
):
    nka, ndev, rows, cols, taps = sizes
    del barrier_send, barrier_recv
    radius = (taps - 1) // 2
    nx = nka // 2
    width = cols // nka
    ext_rows = rows + 2 * radius
    half = rows // 2

    ka = lax.axis_index("ka")
    dev = lax.axis_index("dev")
    x, core = ka // 2, ka % 2
    xs = [lax.rem(x + step, nx) for step in (0, 1, 2, 3)]
    right, left, far = xs[1], xs[3], xs[2]
    to_right = (right * 2 + core, dev)
    to_left = (left * 2 + core, dev)
    to_sib = (x * 2 + 1 - core, dev)
    below = (ka, lax.rem(dev + ndev - 1, ndev))
    above = (ka, lax.rem(dev + 1, ndev))

    order = []
    for place in (far, right, left, x):
        order += [place * 2 + 1 - core, place * 2 + core]

    def columns(chunk):
        return pl.ds(pl.multiple_of(chunk * width, width), width)

    loads = []
    for k, chunk in enumerate(order):
        loads.append(
            (
                pltpu.make_async_copy(fwd.at[0, :, :, columns(chunk)], fwd_buf.at[k], field_sem.at[2 * k]),
                pltpu.make_async_copy(adj.at[0, :, :, columns(chunk)], adj_buf.at[k], field_sem.at[2 * k + 1]),
            )
        )
    block = pl.ds(pl.multiple_of((dev // 2) * 128, 128), 128)
    load_weights = pltpu.make_async_copy(weights, weight_buf, small_sem.at[0])
    load_ids = pltpu.make_async_copy(ids, id_buf, small_sem.at[1])
    load_band = pltpu.make_async_copy(band_t.at[:, block], band_buf, small_sem.at[2])
    load_density = pltpu.make_async_copy(density, ext.at[pl.ds(radius, rows)], small_sem.at[3])
    load_weights.start()
    load_ids.start()
    for pair in loads[:2]:
        for load in pair:
            load.start()
    load_band.start()
    for pair in loads[2:]:
        for load in pair:
            load.start()
    load_density.start()

    barrier = pltpu.get_barrier_semaphore()
    for target in (to_sib, to_right, to_left, below, above):
        pl.semaphore_signal(barrier, inc=1, device_id=target, device_id_type=MESH)
    pl.semaphore_wait(barrier, 5)

    started = []

    def send(src, dst, send_sem, recv_sem, target):
        copy = pltpu.make_async_remote_copy(
            src_ref=src, dst_ref=dst, send_sem=send_sem, recv_sem=recv_sem,
            device_id=target, device_id_type=MESH,
        )
        copy.start()
        started.append(copy)
        return copy

    dens_up = send(
        density.at[pl.ds(rows - radius, radius)], ext.at[pl.ds(0, radius)],
        edge_send.at[0], edge_recv.at[0], above,
    )
    dens_down = send(
        density.at[pl.ds(0, radius)], ext.at[pl.ds(rows + radius, radius)],
        edge_send.at[1], edge_recv.at[1], below,
    )

    load_weights.wait()
    load_ids.wait()
    weight = weight_buf[id_buf[ka]]

    def term(k):
        total = None
        for c in range(6):
            product = fwd_buf[k, c].astype(jnp.float32) * adj_buf[k, c].astype(jnp.float32)
            if total is None:
                total = product
            elif c < 3:
                total = total + product
            else:
                total = total - product
        return weight * total

    pairs = []
    for k in range(8):
        for load in loads[k]:
            load.wait()
        mine[k] = term(k)
        if k % 2 == 0:
            pairs.append(
                send(mine.at[k], pair_in.at[k // 2], pair_send.at[k // 2], pair_recv.at[k // 2], to_sib)
            )

    upper, lower = pl.ds(0, half), pl.ds(half, half)
    pairs[0].wait_recv()
    part[0] = mine[1] + pair_in[0]
    far_right = send(part.at[0, upper], relay_in.at[0], ring_send.at[0], ring_recv.at[0], to_right)
    far_left = send(part.at[0, lower], relay_in.at[1], ring_send.at[1], ring_recv.at[1], to_left)
    pairs[1].wait_recv()
    part[1] = mine[3] + pair_in[1]
    near_right = send(part.at[1, lower], direct_in.at[0, lower], ring_send.at[2], ring_recv.at[2], to_right)
    pairs[2].wait_recv()
    part[2] = mine[5] + pair_in[2]
    near_left = send(part.at[2, upper], direct_in.at[1, upper], ring_send.at[3], ring_recv.at[3], to_left)

    load_band.wait()
    band = band_buf[...]
    band = band / jnp.sum(band, axis=0, keepdims=True)
    band = jnp.concatenate([band, jnp.zeros((128 - taps, 128), jnp.float32)], axis=0)
    band_rows[...] = band.T
    taps_of = band_rows[pl.ds(pl.multiple_of(lax.rem(dev, 2) * rows, rows), rows), :]
    matrix = pltpu.roll(taps_of, 0, 1, stride=1, stride_axis=0)
    high, low = split(matrix)
    high32, low32 = high.astype(jnp.float32), low.astype(jnp.float32)
    stacked = jnp.concatenate([high32, high32, low32, jnp.zeros_like(high32)], axis=0)
    mat_t[...] = stacked.T.astype(jnp.bfloat16)
    mat[:, 0:128] = jnp.concatenate([high32[:, :ext_rows], high32[:, : 128 - ext_rows]], axis=1).astype(jnp.bfloat16)
    mat[:, 128:256] = jnp.concatenate(
        [
            high32[:, 128 - ext_rows : ext_rows],
            low32[:, :ext_rows],
            jnp.zeros((rows, 256 - 3 * ext_rows), jnp.float32),
        ],
        axis=1,
    ).astype(jnp.bfloat16)

    far_right.wait_recv()
    part[1, upper] = part[1, upper] + relay_in[0]
    sum_right = send(part.at[1, upper], direct_in.at[0, upper], ring_send.at[4], ring_recv.at[4], to_right)
    far_left.wait_recv()
    part[2, lower] = part[2, lower] + relay_in[1]
    sum_left = send(part.at[2, lower], direct_in.at[1, lower], ring_send.at[5], ring_recv.at[5], to_left)

    load_density.wait()
    dens_up.wait_recv()
    dens_down.wait_recv()
    first = jnp.where(dev == 0, 0.0, 1.0)
    last = jnp.where(dev == ndev - 1, 0.0, 1.0)
    quot = jnp.tanh(jnp.float32(BETA * ETA)) + jnp.tanh(jnp.float32(BETA * (1.0 - ETA)))
    shift = jnp.tanh(jnp.float32(BETA * ETA))
    ext[pl.ds(0, radius)] = ext[pl.ds(0, radius)] * first
    ext[pl.ds(rows + radius, radius)] = ext[pl.ds(rows + radius, radius)] * last
    for chunk in range(nka):
        at = slice(chunk * width, (chunk + 1) * width)
        high, low = split(ext[:, at])
        operand = jnp.concatenate(
            [high, low, high, jnp.zeros((256 - 3 * ext_rows, width), jnp.bfloat16)], axis=0
        )
        filtered = jnp.dot(mat[...], operand, preferred_element_type=jnp.float32)
        inner = jnp.tanh(BETA * (filtered - ETA))
        projected[:, at] = (shift + inner) / quot
        inner_buf[chunk] = inner
    inner = inner_buf[ka]
    slope = BETA * (1.0 - inner * inner) / quot

    pairs[3].wait_recv()
    sens = mine[7] + pair_in[3]
    near_right.wait_recv()
    near_left.wait_recv()
    sum_right.wait_recv()
    sum_left.wait_recv()
    sens = sens + direct_in[0] + direct_in[1]
    grad = 11.1 * slope * sens

    high, low = split(grad)
    operand = jnp.concatenate([high, low, high, jnp.zeros_like(high)], axis=0)
    spread = jnp.dot(mat_t[0:ext_rows, :], operand, preferred_element_type=jnp.float32)
    halo_out[0] = spread[0:radius]
    halo_out[1] = spread[rows + radius :]
    halo_down = send(halo_out.at[0], halo_in.at[1], edge_send.at[2], edge_recv.at[2], below)
    halo_up = send(halo_out.at[1], halo_in.at[0], edge_send.at[3], edge_recv.at[3], above)

    edge, inside = 2 * radius, rows - 2 * radius
    gather[ka, edge:rows] = spread[2 * radius : rows]
    parts = (
        (pl.ds(edge, inside), pl.ds(edge, inside // 2), pl.ds(edge + inside // 2, inside // 2)),
        (pl.ds(0, edge), pl.ds(0, edge // 2), pl.ds(edge // 2, edge // 2)),
    )

    def hand(chunk, rows_at, slot, target):
        return send(
            gather.at[chunk, rows_at], gather.at[chunk, rows_at], out_send.at[slot], out_recv.at[slot], target
        )

    def own(p, base):
        whole = parts[p][0]
        return (
            hand(ka, whole, base, to_right),
            hand(ka, whole, base + 1, to_left),
            hand(ka, whole, base + 2, to_sib),
        )

    first_out = own(0, 0)
    halo_up.wait_recv()
    halo_down.wait_recv()
    gather[ka, 0:radius] = spread[radius : 2 * radius] + halo_in[0] * first
    gather[ka, radius:edge] = spread[rows : rows + radius] + halo_in[1] * last
    second_out = own(1, 9)

    from_left, from_right, from_far = left * 2 + core, right * 2 + core, far * 2 + core
    relays = []
    for p, (outs, base) in enumerate(((first_out, 0), (second_out, 9))):
        whole, one, two = parts[p]
        outs[0].wait_recv()
        relay_right = hand(from_left, one, base + 3, to_right)
        sib_left = hand(from_left, whole, base + 5, to_sib)
        outs[1].wait_recv()
        relay_left = hand(from_right, two, base + 4, to_left)
        sib_right = hand(from_right, whole, base + 6, to_sib)
        relays.append((relay_right, relay_left, sib_left, sib_right))
    done = []
    for p, (relay, base) in enumerate(zip(relays, (0, 9))):
        whole, one, two = parts[p]
        relay[0].wait_recv()
        done.append(hand(from_far, one, base + 7, to_sib))
        relay[1].wait_recv()
        done.append(hand(from_far, two, base + 8, to_sib))

    def place(chunk):
        at = columns(chunk)
        design[0:radius, at] = gather[chunk, 0:radius]
        design[radius : rows - radius, at] = gather[chunk, edge:rows]
        design[rows - radius : rows, at] = gather[chunk, radius:edge]

    for chunk in (ka, from_left, from_right, from_far):
        place(chunk)
    first_out[2].wait_recv()
    second_out[2].wait_recv()
    place(x * 2 + 1 - core)
    for relay in relays:
        relay[2].wait_recv()
        relay[3].wait_recv()
    place(left * 2 + 1 - core)
    place(right * 2 + 1 - core)
    for copy in done:
        copy.wait_recv()
    place(far * 2 + 1 - core)

    for copy in started:
        copy.wait_send()


def solution(mesh):
    nka, ndev = mesh.shape["ka"], mesh.shape["dev"]

    def shards(density, fields_fwd, fields_adj, filter_band, k_weights, kpoint_ids):
        rows, cols = density.shape
        taps = filter_band.shape[1]
        radius = (taps - 1) // 2
        width = cols // nka
        ext_rows = rows + 2 * radius
        f32, bf16 = jnp.float32, jnp.bfloat16
        in_hbm = pl.BlockSpec(memory_space=pltpu.HBM)
        in_vmem = pl.BlockSpec(memory_space=pltpu.VMEM)
        dma = pltpu.SemaphoreType.DMA
        projected, design = pl.pallas_call(
            functools.partial(kernel, (nka, ndev, rows, cols, taps)),
            out_shape=[jax.ShapeDtypeStruct((rows, cols), f32)] * 2,
            in_specs=[in_hbm] * 6,
            out_specs=[in_vmem] * 2,
            scratch_shapes=[
                pltpu.VMEM((nka, 6, rows, width), bf16),
                pltpu.VMEM((nka, 6, rows, width), bf16),
                pltpu.VMEM((ext_rows, cols), f32),
                pltpu.VMEM((taps, 128), f32),
                pltpu.VMEM((128, 128), f32),
                pltpu.VMEM((rows, 256), bf16),
                pltpu.VMEM((128, 256), bf16),
                pltpu.VMEM((nka, rows, width), f32),
                pltpu.SMEM(k_weights.shape, f32),
                pltpu.SMEM(kpoint_ids.shape, jnp.int32),
                pltpu.VMEM((8, rows, width), f32),
                pltpu.VMEM((4, rows, width), f32),
                pltpu.VMEM((3, rows, width), f32),
                pltpu.VMEM((2, rows // 2, width), f32),
                pltpu.VMEM((2, rows, width), f32),
                pltpu.VMEM((2, radius, width), f32),
                pltpu.VMEM((2, radius, width), f32),
                pltpu.VMEM((nka, rows, width), f32),
                dma((16,)),
                dma((4,)),
                dma((1,)),
                dma((1,)),
                dma((4,)),
                dma((4,)),
                dma((6,)),
                dma((6,)),
                dma((4,)),
                dma((4,)),
                dma((18,)),
                dma((18,)),
            ],
            compiler_params=pltpu.CompilerParams(
                collective_id=0, has_side_effects=True, vmem_limit_bytes=40 * 1024 * 1024
            ),
            name="sensitivities",
        )(
            *(
                pltpu.with_memory_space_constraint(operand, pltpu.HBM)
                for operand in (density, fields_fwd, fields_adj, filter_band.T, k_weights, kpoint_ids)
            )
        )
        return projected, design

    return jax.shard_map(
        shards,
        mesh=mesh,
        in_specs=(
            P("dev", None),
            P("ka", None, "dev", None),
            P("ka", None, "dev", None),
            P(),
            P(),
            P(),
        ),
        out_specs=(P("dev", None), P("dev", None)),
        check_vma=False,
    )
```

time: 119 us -> 35.8 us (0.30)
  the two profiles are of different devices: /device:TPU:120 before, /device:TPU:1 now
where the time goes in v1:
time: 35.8 us; the launch traced here: 35.7 us
  Pallas kernels  33.4 us (93%)
  local copies, waits for them, and re-layouts  1.59 us (4%)
  between operations  0.64 us (2%)
    pallas_call x1, Pallas kernels, shards(): pl.pallas_call(functools.partial(kernel, (nka, ndev, rows, cols, taps)),...  33.4 us
    unnamed x2, local copies, waits for them, and re-layouts  1.59 us

profile of v1, /device:TPU:1, one launch (start us, length us, event | category | flops | bytes accessed | tf_op | source)
XLA Modules:
  0.0 35.7 jit_solution(513528610966922891)
XLA Ops:
  0.6 33.4 %sensitivities.1 = (f32[64,2048]{1,0:T(8,128)S(1)}, f32[64,2048]{1,0:T(8,128)S(1)}) custom-call(f32[64,2048]{1,0:T(8,128)} %density.1, bf16[1,6,64,2048]{3,2,1,0:T(8,128)(2,1)} %fwd.1, bf16[1,6,64,2048]{3,2,1,0:T(8,128)(2,1)} %adj.1, f32[17,4096]{1,0:T(8,128)} %bitcast.1, f32[8]{0:T(128)} %weights.1, s32[8]{0:T(128)} %ids.1), custom_call_target="tpu_custom_call" | custom-call | tf_op jit(solution)/shard_map/sensitivities/pallas_call | solution.py:292
  34.1 0.8 %copy.10 = f32[64,2048]{1,0:T(8,128)} copy(f32[64,2048]{1,0:T(8,128)S(1)} %get-tuple-element.4) | data formatting | bytes 1048576
  34.9 0.8 %copy.11 = f32[64,2048]{1,0:T(8,128)} copy(f32[64,2048]{1,0:T(8,128)S(1)} %get-tuple-element.5) | data formatting | bytes 1048576

commit v2 on v0

v2 whole, which is shorter than its diff:
```python
import functools

import jax
import jax.numpy as jnp
from jax import lax
from jax.experimental import pallas as pl
from jax.experimental.pallas import tpu as pltpu
from jax.sharding import PartitionSpec as P

MESH = pl.DeviceIdType.MESH
BETA, ETA = 8.0, 0.5
F32, BF16 = jnp.float32, jnp.bfloat16


def split(value):
    high = value.astype(BF16)
    low = (value - high.astype(F32)).astype(BF16)
    return high, low


def kernel(
    sizes,
    density, fwd, adj, band_t, weights, ids,
    projected, design,
    fields, terms, pair_in, part, sum_in, edge_in,
    ext, dens_cols, band_buf, band_rows, mat, mat_wide, mat_t, mat_edge, weight_buf, id_buf, inner_rows, end_rows,
    load_sem, small_sem, ready, pair_send, pair_recv, sum_send, sum_recv,
    dens_send, dens_recv, edge_send, edge_recv, out_send, out_recv,
):
    nka, ndev, rows, cols, taps = sizes
    radius = (taps - 1) // 2
    nx = nka // 2
    half = cols // 2
    width = half // nka
    ext_rows = rows + 2 * radius
    side = 2 * radius

    ka = lax.axis_index("ka")
    dev = lax.axis_index("dev")
    x, core = ka // 2, lax.rem(ka, 2)
    mine = core * nx + x
    xs = [lax.rem(x + step, nx) for step in range(nx)]
    sib = (x * 2 + 1 - core, dev)
    line = [(xs[step] * 2 + core, dev) for step in range(nx)]
    dev_up, dev_down = lax.rem(dev + 1, ndev), lax.rem(dev + ndev - 1, ndev)
    up = [(xs[step] * 2 + core, dev_up) for step in range(nx)]
    down = [(xs[step] * 2 + core, dev_down) for step in range(nx)]
    has_up, has_down = dev < ndev - 1, dev > 0
    even_up, even_down = has_up & (lax.rem(dev, 16) == 15), has_down & (lax.rem(dev, 16) == 0)
    early_up = has_up & (lax.rem(dev, 4) != 3)
    early_down = has_down & (lax.rem(dev, 4) == 0) & (lax.rem(dev, 16) != 0)
    late_up, late_down = has_up & ~early_up, has_down & ~early_down

    def columns(h, chunk):
        return pl.ds(pl.multiple_of(h * half + chunk * width, width), width)

    def load(src, dst, sem):
        copy = pltpu.make_async_copy(src, dst, sem)
        copy.start()
        return copy

    def arrived(ref, sem):
        pltpu.make_async_copy(ref, ref, sem).wait()

    def chunks(h, which):
        return pl.ds(pl.multiple_of(h * half + which * nx * width, nx * width), nx * width)

    def load_chunks(h, which, sem):
        at = chunks(h, which)
        load(fwd.at[0, :, :, at], fields.at[0, :, :, at], load_sem.at[sem])
        load(adj.at[0, :, :, at], fields.at[1, :, :, at], load_sem.at[sem])

    small = [
        load(weights, weight_buf, small_sem.at[0]),
        load(ids, id_buf, small_sem.at[1]),
    ]
    load_chunks(0, 1 - core, 0)
    load_chunks(0, core, 1)
    first_band = lax.max(dev * rows - radius, 0) // 128
    last_band = lax.min((dev * rows - radius + 128) // 128, (ndev * rows - 1) // 128)
    for n, block in enumerate((first_band, last_band)):
        load(band_t.at[:, pl.ds(pl.multiple_of(block * 128, 128), 128)], band_buf.at[n], small_sem.at[2])
    load_chunks(1, 1 - core, 2)
    load_chunks(1, core, 3)
    own_rows = pl.ds(side, rows)
    for h in range(2):
        load(density.at[:, columns(h, mine)], dens_cols.at[h, own_rows], small_sem.at[3])
    load_density = load(density, ext.at[pl.ds(radius, rows)], small_sem.at[4])

    barrier = pltpu.get_barrier_semaphore()

    def greet(semaphore, targets):
        for target in targets:
            pl.semaphore_signal(semaphore, inc=1, device_id=target, device_id_type=MESH)

    greet(barrier, [sib] + line[1:])

    @pl.when(early_up | even_up)
    def _():
        greet(barrier, up)

    @pl.when(early_down | even_down)
    def _():
        greet(barrier, down)

    def remote(src, dst, send_sem, recv_sem, target):
        return pltpu.make_async_remote_copy(
            src_ref=src, dst_ref=dst, send_sem=send_sem, recv_sem=recv_sem,
            device_id=target, device_id_type=MESH,
        )

    @pl.when(dev == 0)
    def _():
        ext[pl.ds(0, radius)] = jnp.zeros((radius, cols), F32)
        dens_cols[:, pl.ds(0, side)] = jnp.zeros((2, side, width), F32)
        edge_in[0] = jnp.zeros((nx, 2, radius, width), F32)

    @pl.when(dev == ndev - 1)
    def _():
        ext[pl.ds(radius + rows, radius)] = jnp.zeros((radius, cols), F32)
        dens_cols[:, pl.ds(side + rows, side)] = jnp.zeros((2, side, width), F32)
        edge_in[1] = jnp.zeros((nx, 2, radius, width), F32)

    for copy in small:
        copy.wait()
    weight = weight_buf[id_buf[ka]]

    def fill_terms(h, which, sem):
        arrived(fields.at[:, :, :, chunks(h, which)], load_sem.at[sem])
        for quarter in range(nx):
            at = columns(h, which * nx + quarter)
            total = None
            for c in range(6):
                product = fields[0, c, :, at].astype(F32) * fields[1, c, :, at].astype(F32)
                total = product if total is None else total + product if c < 3 else total - product
            terms[h, which, quarter] = weight * total

    pairs = [
        [
            remote(
                terms.at[h, 1 - core, xs[step]], pair_in.at[h, xs[step]],
                pair_send.at[0], pair_recv.at[h * nx + n], sib,
            )
            for n, step in enumerate((2, 1, 3, 0))
        ]
        for h in range(2)
    ]
    fill_terms(0, 1 - core, 0)

    one = jnp.int32(1)
    greeted = nx + nx * (jnp.where(late_down, one, 0) + jnp.where(late_up, one, 0))
    pl.semaphore_wait(barrier, greeted)

    @pl.when(late_down & ~even_down)
    def _():
        greet(ready.at[0], down)

    @pl.when(late_up & ~even_up)
    def _():
        greet(ready.at[1], up)

    for copy in pairs[0]:
        copy.start()

    first_side, last_side = pl.ds(0, side), pl.ds(rows - side, side)
    cols_down = [
        remote(
            density.at[first_side, columns(h, mine)], dens_cols.at[h, pl.ds(side + rows, side)],
            dens_send.at[0], dens_recv.at[0], down[0],
        )
        for h in range(2)
    ]
    cols_up = [
        remote(
            density.at[last_side, columns(h, mine)], dens_cols.at[h, first_side],
            dens_send.at[1], dens_recv.at[1], up[0],
        )
        for h in range(2)
    ]
    rows_down = remote(
        density.at[pl.ds(0, radius)], ext.at[pl.ds(radius + rows, radius)], dens_send.at[2], dens_recv.at[2], down[0]
    )
    rows_up = remote(
        density.at[pl.ds(rows - radius, radius)], ext.at[pl.ds(0, radius)], dens_send.at[3], dens_recv.at[3], up[0]
    )

    edges_down = [
        remote(part.at[:, xs[s], pl.ds(0, radius)], edge_in.at[1, s], edge_send.at[0], edge_recv.at[0], down[s])
        for s in range(nx)
    ]
    edges_up = [
        remote(
            part.at[:, xs[s], pl.ds(rows - radius, radius)], edge_in.at[0, s],
            edge_send.at[1], edge_recv.at[1], up[s],
        )
        for s in range(nx)
    ]

    @pl.when(late_down)
    def _():
        for copy in cols_down:
            copy.start()

    @pl.when(late_up)
    def _():
        for copy in cols_up:
            copy.start()

    fill_terms(0, core, 1)
    fill_terms(1, 1 - core, 2)
    for copy in pairs[1]:
        copy.start()
    for h in range(2):
        if h == 1:
            fill_terms(1, core, 3)
        for n, step in enumerate((2, 1, 3, 0)):
            pairs[h][n].wait_recv()
            part[h, xs[step]] = terms[h, core, xs[step]] + pair_in[h, xs[step]]
            if step:
                remote(
                    part.at[h, xs[step]], sum_in.at[h, step - 1], sum_send.at[0], sum_recv.at[h], line[step]
                ).start()
        if h == 1:

            @pl.when(late_down)
            def _():
                for copy in edges_down:
                    copy.start()

            @pl.when(late_up)
            def _():
                for copy in edges_up:
                    copy.start()

    @pl.when(late_down)
    def _():
        rows_down.start()

    @pl.when(late_up)
    def _():
        rows_up.start()

    arrived(band_buf, small_sem.at[2])
    for n in range(2):
        band = band_buf[n]
        band = band / jnp.sum(band, axis=0, keepdims=True)
        band = jnp.concatenate([band, jnp.zeros((128 - taps, 128), F32)], axis=0)
        band_rows[n * 128 : (n + 1) * 128] = band.T
    offset = jnp.where(lax.rem(dev, 2) == 0, 128 - radius, rows - radius)
    band_ext = band_rows[pl.ds(pl.multiple_of(offset, radius), ext_rows), :]

    def shear(value, shift):
        return pltpu.roll(value, shift, 1, stride=1, stride_axis=0)

    def parts_of(value):
        high, low = split(value)
        return high.astype(F32), low.astype(F32)

    high, low = parts_of(shear(band_ext, 0))
    mat_wide[:, 0:128] = high.astype(BF16)
    mat_wide[:, 128:256] = high.astype(BF16)
    mat_wide[:, 256:384] = low.astype(BF16)
    high, low = parts_of(shear(band_ext, 128 - 2 * radius))
    stacked = jnp.concatenate([high, high, low, jnp.zeros((256 - 3 * ext_rows, 128), F32)], axis=0).T
    mat_t[...] = stacked[0:rows].astype(BF16)
    mat_edge[...] = jnp.concatenate([stacked[0:radius], stacked[rows - radius : rows]], axis=0).astype(BF16)
    high, low = parts_of(shear(band_ext[radius : radius + rows], 0))
    mat[:, 0:128] = jnp.concatenate([high[:, :ext_rows], high[:, : 128 - ext_rows]], axis=1).astype(BF16)
    mat[:, 128:256] = jnp.concatenate(
        [high[:, 128 - ext_rows : ext_rows], low[:, :ext_rows], jnp.zeros((rows, 256 - 3 * ext_rows), F32)], axis=1
    ).astype(BF16)

    @pl.when(early_up)
    def _():
        pl.semaphore_wait(ready.at[0], nx)
        for copy in cols_up + edges_up + [rows_up]:
            copy.start()

    @pl.when(early_down)
    def _():
        pl.semaphore_wait(ready.at[1], nx)
        for copy in cols_down + edges_down + [rows_down]:
            copy.start()

    quot = jnp.tanh(jnp.float32(BETA * ETA)) + jnp.tanh(jnp.float32(BETA * (1.0 - ETA)))
    shift = jnp.tanh(jnp.float32(BETA * ETA))
    arrived(dens_cols.at[:, own_rows], small_sem.at[3])
    upper_side = pl.ds(side + rows, side)

    @pl.when(has_down)
    def _():
        arrived(dens_cols.at[:, first_side], dens_recv.at[1])

    @pl.when(has_up)
    def _():
        arrived(dens_cols.at[:, upper_side], dens_recv.at[0])

    high, low = split(jnp.concatenate([dens_cols[0], dens_cols[1]], axis=1))
    gap = jnp.zeros((128 - ext_rows - 2 * radius, 2 * width), BF16)
    operand = jnp.concatenate([high, gap, low, gap, high, gap], axis=0)
    filtered = jnp.dot(mat_wide[...], operand, preferred_element_type=F32)
    inner = jnp.tanh(BETA * (filtered - ETA))
    slope = 11.1 * BETA * (1.0 - inner * inner) / quot

    def transposed(matrix, value):
        high, low = split(value)
        pad = jnp.zeros((256 - 3 * ext_rows, value.shape[1]), BF16)
        return jnp.dot(matrix, jnp.concatenate([high, low, high, pad], axis=0), preferred_element_type=F32)

    def hand(buffer, slot, target):
        remote(buffer, buffer, out_send.at[slot // 2], out_recv.at[slot], target).start()

    chip = pl.ds(core * nx, nx)
    three = pl.ds(0, nx - 1)
    none = jnp.zeros((radius, width), F32)
    grads = []
    for h in range(2):
        arrived(sum_in.at[h], sum_recv.at[h])
        sens = (part[h, x] + sum_in[h, 0]) + (sum_in[h, 1] + sum_in[h, 2])
        grads.append(slope[radius : radius + rows, h * width : (h + 1) * width] * sens)
        own = transposed(mat_t[...], jnp.concatenate([none, grads[h], none], axis=0))
        inner_rows[h, mine] = own[radius : rows - radius]
        for step in (2, 1, 3):
            hand(inner_rows.at[h, mine], h, line[step])

    @pl.when(has_up)
    def _():
        arrived(edge_in.at[1], edge_recv.at[0])

    @pl.when(has_down)
    def _():
        arrived(edge_in.at[0], edge_recv.at[1])

    edge = edge_in[:, 0] + edge_in[:, 1] + (edge_in[:, 2] + edge_in[:, 3])
    first, last = [jnp.concatenate([edge[n, 0], edge[n, 1]], axis=1) for n in range(2)]
    grad = jnp.concatenate(
        [slope[0:radius] * first, jnp.concatenate(grads, axis=1), slope[radius + rows :] * last], axis=0
    )
    ends = transposed(mat_edge[...], grad)
    for h in range(2):
        end_rows[mine, h] = ends[:, h * width : (h + 1) * width]
    for step in (2, 1, 3):
        hand(end_rows.at[mine], 4, line[step])

    load_density.wait()

    @pl.when(has_down)
    def _():
        rows_up.wait_recv()

    @pl.when(has_up)
    def _():
        rows_down.wait_recv()

    for chunk in range(8):
        at = slice(chunk * cols // 8, (chunk + 1) * cols // 8)
        high, low = split(ext[:, at])
        pad = jnp.zeros((256 - 3 * ext_rows, cols // 8), BF16)
        operand = jnp.concatenate([high, low, high, pad], axis=0)
        filtered = jnp.dot(mat[...], operand, preferred_element_type=F32)
        projected[:, at] = (shift + jnp.tanh(BETA * (filtered - ETA))) / quot

    for h in range(2):
        arrived(inner_rows.at[h, three], out_recv.at[h])
        hand(inner_rows.at[h, chip], 2 + h, sib)
    arrived(end_rows.at[three], out_recv.at[4])
    hand(end_rows.at[chip], 6, sib)

    def place_inner(h, which):
        for quarter in range(nx):
            chunk = which * nx + quarter
            design[radius : rows - radius, columns(h, chunk)] = inner_rows[h, chunk]

    def place_ends(which):
        for quarter in range(nx):
            chunk = which * nx + quarter
            for h in range(2):
                design[0:radius, columns(h, chunk)] = end_rows[chunk, h, 0:radius]
                design[rows - radius : rows, columns(h, chunk)] = end_rows[chunk, h, radius:side]

    for h in range(2):
        place_inner(h, core)
    place_ends(core)
    other = pl.ds((1 - core) * nx, nx)
    for h in range(2):
        arrived(inner_rows.at[h, other], out_recv.at[2 + h])
        place_inner(h, 1 - core)
    arrived(end_rows.at[other], out_recv.at[6])
    place_ends(1 - core)

    arrived(pair_in, pair_send.at[0])
    arrived(sum_in, sum_send.at[0])
    arrived(inner_rows.at[:, three], out_send.at[0])
    arrived(inner_rows.at[:, chip], out_send.at[1])
    arrived(end_rows.at[three], out_send.at[2])
    arrived(end_rows.at[chip], out_send.at[3])

    @pl.when(has_down)
    def _():
        arrived(dens_cols.at[:, first_side], dens_send.at[0])
        rows_down.wait_send()
        arrived(edge_in.at[1], edge_send.at[0])

    @pl.when(has_up)
    def _():
        arrived(dens_cols.at[:, first_side], dens_send.at[1])
        rows_up.wait_send()
        arrived(edge_in.at[0], edge_send.at[1])


def write(projected, design, projected_out, design_out, sem):
    copies = [
        pltpu.make_async_copy(projected, projected_out, sem.at[0]),
        pltpu.make_async_copy(design, design_out, sem.at[1]),
    ]
    for copy in copies:
        copy.start()
    for copy in copies:
        copy.wait()


def solution(mesh):
    nka, ndev = mesh.shape["ka"], mesh.shape["dev"]

    def shards(density, fields_fwd, fields_adj, filter_band, k_weights, kpoint_ids):
        rows, cols = density.shape
        taps = filter_band.shape[1]
        radius = (taps - 1) // 2
        nx, width = nka // 2, cols // 2 // nka
        ext_rows = rows + 2 * radius
        in_vmem = pl.BlockSpec(memory_space=pltpu.VMEM)
        dma = pltpu.SemaphoreType.DMA
        results = pl.pallas_call(
            functools.partial(kernel, (nka, ndev, rows, cols, taps)),
            out_shape=[jax.ShapeDtypeStruct((rows, cols), F32)] * 2,
            in_specs=[pl.BlockSpec(memory_space=pltpu.HBM)] * 6,
            out_specs=[in_vmem] * 2,
            scratch_shapes=[
                pltpu.VMEM((2, 6, rows, cols), BF16),
                pltpu.VMEM((2, 2, nx, rows, width), F32),
                pltpu.VMEM((2, nx, rows, width), F32),
                pltpu.VMEM((2, nx, rows, width), F32),
                pltpu.VMEM((2, nx - 1, rows, width), F32),
                pltpu.VMEM((2, nx, 2, radius, width), F32),
                pltpu.VMEM((ext_rows, cols), F32),
                pltpu.VMEM((2, ext_rows + 2 * radius, width), F32),
                pltpu.VMEM((2, taps, 128), F32),
                pltpu.VMEM((256, 128), F32),
                pltpu.VMEM((rows, 256), BF16),
                pltpu.VMEM((ext_rows, 384), BF16),
                pltpu.VMEM((rows, 256), BF16),
                pltpu.VMEM((2 * radius, 256), BF16),
                pltpu.SMEM(k_weights.shape, F32),
                pltpu.SMEM(kpoint_ids.shape, jnp.int32),
                pltpu.VMEM((2, nka, rows - 2 * radius, width), F32),
                pltpu.VMEM((nka, 2, 2 * radius, width), F32),
                dma((4,)),
                dma((5,)),
                pltpu.SemaphoreType.REGULAR((2,)),
                dma((1,)),
                dma((2 * nx,)),
                dma((1,)),
                dma((2,)),
                dma((4,)),
                dma((4,)),
                dma((2,)),
                dma((2,)),
                dma((4,)),
                dma((7,)),
            ],
            compiler_params=pltpu.CompilerParams(
                collective_id=0, has_side_effects=True, vmem_limit_bytes=40 * 1024 * 1024
            ),
            name="sensitivities",
        )(
            *(
                pltpu.with_memory_space_constraint(operand, pltpu.HBM)
                for operand in (density, fields_fwd, fields_adj, filter_band.T, k_weights, kpoint_ids)
            )
        )
        return pl.pallas_call(
            write,
            out_shape=[jax.ShapeDtypeStruct((rows, cols), F32)] * 2,
            in_specs=[in_vmem] * 2,
            out_specs=[pl.BlockSpec(memory_space=pltpu.HBM)] * 2,
            scratch_shapes=[dma((2,))],
            name="write_results",
        )(*(pltpu.with_memory_space_constraint(result, pltpu.VMEM) for result in results))

    return jax.shard_map(
        shards,
        mesh=mesh,
        in_specs=(
            P("dev", None),
            P("ka", None, "dev", None),
            P("ka", None, "dev", None),
            P(),
            P(),
            P(),
        ),
        out_specs=(P("dev", None), P("dev", None)),
        check_vma=False,
    )
```

time: 119 us -> 23.3 us (0.20)
  the two profiles are of different devices: /device:TPU:120 before, /device:TPU:1 now
where the time goes in v2:
time: 23.3 us; the launch traced here: 23.2 us
  Pallas kernels  22.6 us (97%)
  between operations  0.64 us (3%)
    pallas_call x1, Pallas kernels, shards(): pl.pallas_call(functools.partial(kernel, (nka, ndev, rows, cols, taps)),...  21.6 us
    pallas_call x1, Pallas kernels, shards(): pl.pallas_call(write, out_shape=[jax.ShapeDtypeStruct((rows, cols), F32)]...  0.99 us

profile of v2, /device:TPU:1, one launch (start us, length us, event | category | flops | bytes accessed | tf_op | source)
XLA Modules:
  0.0 23.2 jit_solution(18190911651036184100)
XLA Ops:
  0.6 21.6 %sensitivities.1 = (f32[64,2048]{1,0:T(8,128)S(1)}, f32[64,2048]{1,0:T(8,128)S(1)}) custom-call(f32[64,2048]{1,0:T(8,128)} %density.1, bf16[1,6,64,2048]{3,2,1,0:T(8,128)(2,1)} %fwd.1, bf16[1,6,64,2048]{3,2,1,0:T(8,128)(2,1)} %adj.1, f32[17,4096]{1,0:T(8,128)} %bitcast.1, f32[8]{0:T(128)} %weights.1, s32[8]{0:T(128)} %ids.1), custom_call_target="tpu_custom_call" | custom-call | tf_op jit(solution)/shard_map/sensitivities/pallas_call | solution.py:433
  22.2 1.0 %write_results.1 = (f32[64,2048]{1,0:T(8,128)}, f32[64,2048]{1,0:T(8,128)}) custom-call(f32[64,2048]{1,0:T(8,128)S(1)} %get-tuple-element.4.projected, f32[64,2048]{1,0:T(8,128)S(1)} %get-tuple-element.5.design), custom_call_target="tpu_custom_call" | custom-call | tf_op jit(solution)/shard_map/write_results/pallas_call | solution.py:481

commit v3 on v2

--- a/solution.py
+++ b/solution.py
@@ -46,10 +46,12 @@
     up = [(xs[step] * 2 + core, dev_up) for step in range(nx)]
     down = [(xs[step] * 2 + core, dev_down) for step in range(nx)]
     has_up, has_down = dev < ndev - 1, dev > 0
-    even_up, even_down = has_up & (lax.rem(dev, 16) == 15), has_down & (lax.rem(dev, 16) == 0)
-    early_up = has_up & (lax.rem(dev, 4) != 3)
-    early_down = has_down & (lax.rem(dev, 4) == 0) & (lax.rem(dev, 16) != 0)
+    even_up, even_down = has_up & ((dev == 15) | (dev == 31)), has_down & ((dev == 16) | (dev == 32))
+    early_up = has_up & (lax.rem(dev, 4) != 3) & (dev != 0)
+    early_down = has_down & ((lax.rem(dev, 4) == 0) | (dev == 1)) & ~even_down
     late_up, late_down = has_up & ~early_up, has_down & ~early_down
+    late_chip = jnp.where(dev == 0, 0, nx // 2)
+    is_late = x == late_chip
 
     def columns(h, chunk):
         return pl.ds(pl.multiple_of(h * half + chunk * width, width), width)
@@ -76,32 +78,55 @@
     ]
     load_chunks(0, 1 - core, 0)
     load_chunks(0, core, 1)
+    load_chunks(1, 1 - core, 2)
+    load_chunks(1, core, 3)
+
+    barrier = pltpu.get_barrier_semaphore()
+
+    def greet(semaphore, targets):
+        for target in targets:
+            pl.semaphore_signal(semaphore, inc=1, device_id=target, device_id_type=MESH)
+
+    greet(barrier, [sib])
+
+    @pl.when(~is_late)
+    def _():
+        greet(barrier, line[1:])
+
+    @pl.when(early_up | even_up)
+    def _():
+        greet(barrier, up)
+
+    @pl.when(early_down | even_down)
+    def _():
+        greet(barrier, down)
+
+    one = jnp.int32(1)
+    greeted = nx - 1 + jnp.where(is_late, one, 0) + nx * (jnp.where(late_down, one, 0) + jnp.where(late_up, one, 0))
+
+    def answer():
+        @pl.when(late_down & ~even_down)
+        def _():
+            greet(ready.at[0], down)
+
+        @pl.when(late_up & ~even_up)
+        def _():
+            greet(ready.at[1], up)
+
+    @pl.when(is_late)
+    def _():
+        pl.semaphore_wait(barrier, greeted)
+        greet(ready.at[2], line[1:])
+        answer()
+
     first_band = lax.max(dev * rows - radius, 0) // 128
     last_band = lax.min((dev * rows - radius + 128) // 128, (ndev * rows - 1) // 128)
     for n, block in enumerate((first_band, last_band)):
         load(band_t.at[:, pl.ds(pl.multiple_of(block * 128, 128), 128)], band_buf.at[n], small_sem.at[2])
-    load_chunks(1, 1 - core, 2)
-    load_chunks(1, core, 3)
     own_rows = pl.ds(side, rows)
     for h in range(2):
         load(density.at[:, columns(h, mine)], dens_cols.at[h, own_rows], small_sem.at[3])
     load_density = load(density, ext.at[pl.ds(radius, rows)], small_sem.at[4])
-
-    barrier = pltpu.get_barrier_semaphore()
-
-    def greet(semaphore, targets):
-        for target in targets:
-            pl.semaphore_signal(semaphore, inc=1, device_id=target, device_id_type=MESH)
-
-    greet(barrier, [sib] + line[1:])
-
-    @pl.when(early_up | even_up)
-    def _():
-        greet(barrier, up)
-
-    @pl.when(early_down | even_down)
-    def _():
-        greet(barrier, down)
 
     def remote(src, dst, send_sem, recv_sem, target):
         return pltpu.make_async_remote_copy(
@@ -135,32 +160,15 @@
                 total = product if total is None else total + product if c < 3 else total - product
             terms[h, which, quarter] = weight * total
 
-    pairs = [
-        [
-            remote(
-                terms.at[h, 1 - core, xs[step]], pair_in.at[h, xs[step]],
-                pair_send.at[0], pair_recv.at[h * nx + n], sib,
-            )
-            for n, step in enumerate((2, 1, 3, 0))
-        ]
-        for h in range(2)
-    ]
+    pairs = [remote(terms.at[h, 1 - core], pair_in.at[h], pair_send.at[0], pair_recv.at[h], sib) for h in range(2)]
     fill_terms(0, 1 - core, 0)
 
-    one = jnp.int32(1)
-    greeted = nx + nx * (jnp.where(late_down, one, 0) + jnp.where(late_up, one, 0))
-    pl.semaphore_wait(barrier, greeted)
-
-    @pl.when(late_down & ~even_down)
-    def _():
-        greet(ready.at[0], down)
-
-    @pl.when(late_up & ~even_up)
-    def _():
-        greet(ready.at[1], up)
-
-    for copy in pairs[0]:
-        copy.start()
+    @pl.when(~is_late)
+    def _():
+        pl.semaphore_wait(barrier, greeted)
+        answer()
+
+    pairs[0].start()
 
     first_side, last_side = pl.ds(0, side), pl.ds(rows - side, side)
     cols_down = [
@@ -208,18 +216,18 @@
 
     fill_terms(0, core, 1)
     fill_terms(1, 1 - core, 2)
-    for copy in pairs[1]:
-        copy.start()
+    pairs[1].start()
     for h in range(2):
         if h == 1:
             fill_terms(1, core, 3)
-        for n, step in enumerate((2, 1, 3, 0)):
-            pairs[h][n].wait_recv()
+        pairs[h].wait_recv()
+        for step in (2, 1, 3, 0):
             part[h, xs[step]] = terms[h, core, xs[step]] + pair_in[h, xs[step]]
             if step:
-                remote(
+                copy = remote(
                     part.at[h, xs[step]], sum_in.at[h, step - 1], sum_send.at[0], sum_recv.at[h], line[step]
-                ).start()
+                )
+                pl.when(is_late | (xs[step] != late_chip))(copy.start)
         if h == 1:
 
             @pl.when(late_down)
@@ -231,6 +239,15 @@
             def _():
                 for copy in edges_up:
                     copy.start()
+
+    @pl.when(~is_late)
+    def _():
+        pl.semaphore_wait(ready.at[2], 1)
+        slot = lax.rem(late_chip - x + nx, nx) - 1
+        for h in range(2):
+            remote(
+                part.at[h, late_chip], sum_in.at[h, slot], sum_send.at[0], sum_recv.at[h], (late_chip * 2 + core, dev)
+            ).start()
 
     @pl.when(late_down)
     def _():
@@ -409,14 +426,13 @@
 
 
 def write(projected, design, projected_out, design_out, sem):
-    copies = [
-        pltpu.make_async_copy(projected, projected_out, sem.at[0]),
-        pltpu.make_async_copy(design, design_out, sem.at[1]),
-    ]
-    for copy in copies:
-        copy.start()
-    for copy in copies:
-        copy.wait()
+    count = projected.shape[0] // 4
+    for n in range(4):
+        at = pl.ds(n * count, count)
+        pltpu.make_async_copy(projected.at[at], projected_out.at[at], sem.at[0]).start()
+        pltpu.make_async_copy(design.at[at], design_out.at[at], sem.at[1]).start()
+    pltpu.make_async_copy(projected, projected_out, sem.at[0]).wait()
+    pltpu.make_async_copy(design, design_out, sem.at[1]).wait()
 
 
 def solution(mesh):
@@ -456,9 +472,9 @@
                 pltpu.VMEM((nka, 2, 2 * radius, width), F32),
                 dma((4,)),
                 dma((5,)),
-                pltpu.SemaphoreType.REGULAR((2,)),
+                pltpu.SemaphoreType.REGULAR((3,)),
                 dma((1,)),
-                dma((2 * nx,)),
+                dma((2,)),
                 dma((1,)),
                 dma((2,)),
                 dma((4,)),

time: 23.3 us -> 22.4 us (0.961)
  Pallas kernels: 22.6 us -> 21.6 us
    pallas_call x1, Pallas kernels: 21.6 us -> 20.7 us  [shards(): pl.pallas_call(functools.partial(kernel, (nka, ndev, rows, cols, taps)),...]
where the time goes in v3:
time: 22.4 us; the launch traced here: 22.3 us
  Pallas kernels  21.6 us (96%)
  between operations  0.64 us (3%)
    pallas_call x1, Pallas kernels, shards(): pl.pallas_call(functools.partial(kernel, (nka, ndev, rows, cols, taps)),...  20.7 us
    pallas_call x1, Pallas kernels, shards(): pl.pallas_call(write, out_shape=[jax.ShapeDtypeStruct((rows, cols), F32)]...  0.97 us

profile of v3, /device:TPU:1, one launch (start us, length us, event | category | flops | bytes accessed | tf_op | source)
XLA Modules:
  0.0 22.3 jit_solution(17836938512036461408)
XLA Ops:
  0.6 20.7 %sensitivities.1 = (f32[64,2048]{1,0:T(8,128)S(1)}, f32[64,2048]{1,0:T(8,128)S(1)}) custom-call(f32[64,2048]{1,0:T(8,128)} %density.1, bf16[1,6,64,2048]{3,2,1,0:T(8,128)(2,1)} %fwd.1, bf16[1,6,64,2048]{3,2,1,0:T(8,128)(2,1)} %adj.1, f32[17,4096]{1,0:T(8,128)} %bitcast.1, f32[8]{0:T(128)} %weights.1, s32[8]{0:T(128)} %ids.1), custom_call_target="tpu_custom_call" | custom-call | tf_op jit(solution)/shard_map/sensitivities/pallas_call | solution.py:449
  21.3 1.0 %write_results.1 = (f32[64,2048]{1,0:T(8,128)}, f32[64,2048]{1,0:T(8,128)}) custom-call(f32[64,2048]{1,0:T(8,128)S(1)} %get-tuple-element.4.projected, f32[64,2048]{1,0:T(8,128)S(1)} %get-tuple-element.5.design), custom_call_target="tpu_custom_call" | custom-call | tf_op jit(solution)/shard_map/write_results/pallas_call | solution.py:497

commit v4 on v3

--- a/solution.py
+++ b/solution.py
@@ -215,11 +215,8 @@
             copy.start()
 
     fill_terms(0, core, 1)
-    fill_terms(1, 1 - core, 2)
-    pairs[1].start()
-    for h in range(2):
-        if h == 1:
-            fill_terms(1, core, 3)
+
+    def send_sums(h):
         pairs[h].wait_recv()
         for step in (2, 1, 3, 0):
             part[h, xs[step]] = terms[h, core, xs[step]] + pair_in[h, xs[step]]
@@ -228,17 +225,32 @@
                     part.at[h, xs[step]], sum_in.at[h, step - 1], sum_send.at[0], sum_recv.at[h], line[step]
                 )
                 pl.when(is_late | (xs[step] != late_chip))(copy.start)
-        if h == 1:
-
-            @pl.when(late_down)
-            def _():
-                for copy in edges_down:
-                    copy.start()
-
-            @pl.when(late_up)
-            def _():
-                for copy in edges_up:
-                    copy.start()
+
+    latest = (dev == 0) & (ka == 0)
+
+    @pl.when(latest)
+    def _():
+        send_sums(0)
+
+    fill_terms(1, 1 - core, 2)
+    pairs[1].start()
+
+    @pl.when(~latest)
+    def _():
+        send_sums(0)
+
+    fill_terms(1, core, 3)
+    send_sums(1)
+
+    @pl.when(late_down)
+    def _():
+        for copy in edges_down:
+            copy.start()
+
+    @pl.when(late_up)
+    def _():
+        for copy in edges_up:
+            copy.start()
 
     @pl.when(~is_late)
     def _():

time: 22.4 us -> 22.3 us (level)
  no operation moved by 1% of the time
where the time goes in v4:
time: 22.3 us; the launch traced here: 22.2 us
  Pallas kernels  21.5 us (96%)
  between operations  0.64 us (3%)
    pallas_call x1, Pallas kernels, shards(): pl.pallas_call(functools.partial(kernel, (nka, ndev, rows, cols, taps)),...  20.6 us
    pallas_call x1, Pallas kernels, shards(): pl.pallas_call(write, out_shape=[jax.ShapeDtypeStruct((rows, cols), F32)]...  0.97 us

profile of v4, /device:TPU:1, one launch (start us, length us, event | category | flops | bytes accessed | tf_op | source)
XLA Modules:
  0.0 22.2 jit_solution(18388644501262230746)
XLA Ops:
  0.6 20.6 %sensitivities.1 = (f32[64,2048]{1,0:T(8,128)S(1)}, f32[64,2048]{1,0:T(8,128)S(1)}) custom-call(f32[64,2048]{1,0:T(8,128)} %density.1, bf16[1,6,64,2048]{3,2,1,0:T(8,128)(2,1)} %fwd.1, bf16[1,6,64,2048]{3,2,1,0:T(8,128)(2,1)} %adj.1, f32[17,4096]{1,0:T(8,128)} %bitcast.1, f32[8]{0:T(128)} %weights.1, s32[8]{0:T(128)} %ids.1), custom_call_target="tpu_custom_call" | custom-call | tf_op jit(solution)/shard_map/sensitivities/pallas_call | solution.py:461
  21.2 1.0 %write_results.1 = (f32[64,2048]{1,0:T(8,128)}, f32[64,2048]{1,0:T(8,128)}) custom-call(f32[64,2048]{1,0:T(8,128)S(1)} %get-tuple-element.4.projected, f32[64,2048]{1,0:T(8,128)S(1)} %get-tuple-element.5.design), custom_call_target="tpu_custom_call" | custom-call | tf_op jit(solution)/shard_map/write_results/pallas_call | solution.py:509

commit v5 on v4

--- a/solution.py
+++ b/solution.py
@@ -24,8 +24,7 @@
     projected, design,
     fields, terms, pair_in, part, sum_in, edge_in,
     ext, dens_cols, band_buf, band_rows, mat, mat_wide, mat_t, mat_edge, weight_buf, id_buf, inner_rows, end_rows,
-    load_sem, small_sem, ready, pair_send, pair_recv, sum_send, sum_recv,
-    dens_send, dens_recv, edge_send, edge_recv, out_send, out_recv,
+    load_sem, small_sem, ready, sent, pair_recv, sum_recv, dens_recv, edge_recv, out_recv,
 ):
     nka, ndev, rows, cols, taps = sizes
     radius = (taps - 1) // 2
@@ -53,6 +52,14 @@
     late_chip = jnp.where(dev == 0, 0, nx // 2)
     is_late = x == late_chip
 
+    barrier = pltpu.get_barrier_semaphore()
+
+    def greet(semaphore, targets):
+        for target in targets:
+            pl.semaphore_signal(semaphore, inc=1, device_id=target, device_id_type=MESH)
+
+    greet(barrier, [sib])
+
     def columns(h, chunk):
         return pl.ds(pl.multiple_of(h * half + chunk * width, width), width)
 
@@ -72,22 +79,14 @@
         load(fwd.at[0, :, :, at], fields.at[0, :, :, at], load_sem.at[sem])
         load(adj.at[0, :, :, at], fields.at[1, :, :, at], load_sem.at[sem])
 
+    load_chunks(0, 1 - core, 0)
     small = [
         load(weights, weight_buf, small_sem.at[0]),
         load(ids, id_buf, small_sem.at[1]),
     ]
-    load_chunks(0, 1 - core, 0)
     load_chunks(0, core, 1)
     load_chunks(1, 1 - core, 2)
     load_chunks(1, core, 3)
-
-    barrier = pltpu.get_barrier_semaphore()
-
-    def greet(semaphore, targets):
-        for target in targets:
-            pl.semaphore_signal(semaphore, inc=1, device_id=target, device_id_type=MESH)
-
-    greet(barrier, [sib])
 
     @pl.when(~is_late)
     def _():
@@ -160,7 +159,7 @@
                 total = product if total is None else total + product if c < 3 else total - product
             terms[h, which, quarter] = weight * total
 
-    pairs = [remote(terms.at[h, 1 - core], pair_in.at[h], pair_send.at[0], pair_recv.at[h], sib) for h in range(2)]
+    pairs = [remote(terms.at[h, 1 - core], pair_in.at[h], sent.at[0], pair_recv.at[h], sib) for h in range(2)]
     fill_terms(0, 1 - core, 0)
 
     @pl.when(~is_late)
@@ -174,32 +173,32 @@
     cols_down = [
         remote(
             density.at[first_side, columns(h, mine)], dens_cols.at[h, pl.ds(side + rows, side)],
-            dens_send.at[0], dens_recv.at[0], down[0],
+            sent.at[2], dens_recv.at[0], down[0],
         )
         for h in range(2)
     ]
     cols_up = [
         remote(
             density.at[last_side, columns(h, mine)], dens_cols.at[h, first_side],
-            dens_send.at[1], dens_recv.at[1], up[0],
+            sent.at[3], dens_recv.at[1], up[0],
         )
         for h in range(2)
     ]
     rows_down = remote(
-        density.at[pl.ds(0, radius)], ext.at[pl.ds(radius + rows, radius)], dens_send.at[2], dens_recv.at[2], down[0]
+        density.at[pl.ds(0, radius)], ext.at[pl.ds(radius + rows, radius)], sent.at[2], dens_recv.at[2], down[0]
     )
     rows_up = remote(
-        density.at[pl.ds(rows - radius, radius)], ext.at[pl.ds(0, radius)], dens_send.at[3], dens_recv.at[3], up[0]
+        density.at[pl.ds(rows - radius, radius)], ext.at[pl.ds(0, radius)], sent.at[3], dens_recv.at[3], up[0]
     )
 
     edges_down = [
-        remote(part.at[:, xs[s], pl.ds(0, radius)], edge_in.at[1, s], edge_send.at[0], edge_recv.at[0], down[s])
+        remote(part.at[:, xs[s], pl.ds(0, radius)], edge_in.at[1, s], sent.at[2], edge_recv.at[0], down[s])
         for s in range(nx)
     ]
     edges_up = [
         remote(
             part.at[:, xs[s], pl.ds(rows - radius, radius)], edge_in.at[0, s],
-            edge_send.at[1], edge_recv.at[1], up[s],
+            sent.at[3], edge_recv.at[1], up[s],
         )
         for s in range(nx)
     ]
@@ -222,7 +221,7 @@
             part[h, xs[step]] = terms[h, core, xs[step]] + pair_in[h, xs[step]]
             if step:
                 copy = remote(
-                    part.at[h, xs[step]], sum_in.at[h, step - 1], sum_send.at[0], sum_recv.at[h], line[step]
+                    part.at[h, xs[step]], sum_in.at[h, step - 1], sent.at[1], sum_recv.at[h], line[step]
                 )
                 pl.when(is_late | (xs[step] != late_chip))(copy.start)
 
@@ -258,7 +257,7 @@
         slot = lax.rem(late_chip - x + nx, nx) - 1
         for h in range(2):
             remote(
-                part.at[h, late_chip], sum_in.at[h, slot], sum_send.at[0], sum_recv.at[h], (late_chip * 2 + core, dev)
+                part.at[h, late_chip], sum_in.at[h, slot], sent.at[1], sum_recv.at[h], (late_chip * 2 + core, dev)
             ).start()
 
     @pl.when(late_down)
@@ -337,7 +336,7 @@
         return jnp.dot(matrix, jnp.concatenate([high, low, high, pad], axis=0), preferred_element_type=F32)
 
     def hand(buffer, slot, target):
-        remote(buffer, buffer, out_send.at[slot // 2], out_recv.at[slot], target).start()
+        remote(buffer, buffer, sent.at[0 if slot % 4 >= 2 else 1], out_recv.at[slot], target).start()
 
     chip = pl.ds(core * nx, nx)
     three = pl.ds(0, nx - 1)
@@ -417,24 +416,17 @@
     arrived(end_rows.at[other], out_recv.at[6])
     place_ends(1 - core)
 
-    arrived(pair_in, pair_send.at[0])
-    arrived(sum_in, sum_send.at[0])
-    arrived(inner_rows.at[:, three], out_send.at[0])
-    arrived(inner_rows.at[:, chip], out_send.at[1])
-    arrived(end_rows.at[three], out_send.at[2])
-    arrived(end_rows.at[chip], out_send.at[3])
+    arrived(terms, sent.at[0])
+    arrived(terms.at[:, :, pl.ds(0, nx - 1)], sent.at[1])
+    side_bytes = inner_rows.at[:, pl.ds(0, 7), pl.ds(0, 16)]
 
     @pl.when(has_down)
     def _():
-        arrived(dens_cols.at[:, first_side], dens_send.at[0])
-        rows_down.wait_send()
-        arrived(edge_in.at[1], edge_send.at[0])
+        arrived(side_bytes, sent.at[2])
 
     @pl.when(has_up)
     def _():
-        arrived(dens_cols.at[:, first_side], dens_send.at[1])
-        rows_up.wait_send()
-        arrived(edge_in.at[0], edge_send.at[1])
+        arrived(side_bytes, sent.at[3])
 
 
 def write(projected, design, projected_out, design_out, sem):
@@ -485,15 +477,11 @@
                 dma((4,)),
                 dma((5,)),
                 pltpu.SemaphoreType.REGULAR((3,)),
-                dma((1,)),
-                dma((2,)),
-                dma((1,)),
-                dma((2,)),
-                dma((4,)),
                 dma((4,)),
                 dma((2,)),
                 dma((2,)),
                 dma((4,)),
+                dma((2,)),
                 dma((7,)),
             ],
             compiler_params=pltpu.CompilerParams(

time: 22.3 us -> 22.2 us (level)
  no operation moved by 1% of the time
where the time goes in v5:
time: 22.2 us; the launch traced here: 22 us
  Pallas kernels  21.4 us (96%)
  between operations  0.64 us (3%)
    pallas_call x1, Pallas kernels, shards(): pl.pallas_call(functools.partial(kernel, (nka, ndev, rows, cols, taps)),...  20.4 us
    pallas_call x1, Pallas kernels, shards(): pl.pallas_call(write, out_shape=[jax.ShapeDtypeStruct((rows, cols), F32)]...  0.97 us

profile of v5, /device:TPU:1, one launch (start us, length us, event | category | flops | bytes accessed | tf_op | source)
XLA Modules:
  0.0 22.0 jit_solution(5910496171374491084)
XLA Ops:
  0.6 20.4 %sensitivities.1 = (f32[64,2048]{1,0:T(8,128)S(1)}, f32[64,2048]{1,0:T(8,128)S(1)}) custom-call(f32[64,2048]{1,0:T(8,128)} %density.1, bf16[1,6,64,2048]{3,2,1,0:T(8,128)(2,1)} %fwd.1, bf16[1,6,64,2048]{3,2,1,0:T(8,128)(2,1)} %adj.1, f32[17,4096]{1,0:T(8,128)} %bitcast.1, f32[8]{0:T(128)} %weights.1, s32[8]{0:T(128)} %ids.1), custom_call_target="tpu_custom_call" | custom-call | tf_op jit(solution)/shard_map/sensitivities/pallas_call | solution.py:453
  21.1 1.0 %write_results.1 = (f32[64,2048]{1,0:T(8,128)}, f32[64,2048]{1,0:T(8,128)}) custom-call(f32[64,2048]{1,0:T(8,128)S(1)} %get-tuple-element.4.projected, f32[64,2048]{1,0:T(8,128)S(1)} %get-tuple-element.5.design), custom_call_target="tpu_custom_call" | custom-call | tf_op jit(solution)/shard_map/write_results/pallas_call | solution.py:497
